TPU v7x, 512 devices: a whole 4x4x16 slice. The times are simulated.
512 devices in a mesh: group: 8 (over x, core), dev: 64 (over z, y).
Axes of the slice: x: 4, y: 4, z: 16, core: 2. Of those that a mesh axis runs over, the one named last changes fastest.
Arguments:
- cam_jac: float32 [2, 9, 8, 262144], P(None, None, None, ('group', 'dev')), may hold values from -6 to 6
- lm_jac: float32 [2, 3, 8, 262144], P(None, None, None, ('group', 'dev')), may hold values from -6 to 6
- resid: float32 [2, 8, 262144], P(None, None, ('group', 'dev')), may hold values from -6 to 6
- cam_index: int32 [8, 262144], P(None, ('group', 'dev')), may hold values from 0 to 8191
Outputs:
- camera_step: float32 [9, 8192], P(None, 'dev')
- camera_residual: float32 [9, 8192], P(None, 'dev')
- landmark_step: float32 [3, 262144], P(None, ('group', 'dev'))
Inputs may be any that keep to these rules, and one draw needn't show every extreme that they name: `cam_index`: every observation names one of the 8192 cameras.
All inputs are finite; a program needn't handle non-finite values.
Results may differ from a plain program's by a relative error of at most 0.0003.
Values sent between devices are 32-bit elements; how exact they have to be, the bound alone decides.
A program may use at most 64 MiB of HBM per device.

v0:
```python
import jax
import jax.numpy as jnp
from jax import lax
from jax.sharding import PartitionSpec as P

CAM_DEV = 128
ITERS = 2
DAMPING = 1.0


def landmark_inverse(lm_jac):

    def entry(first, second):
        return jnp.sum(lm_jac[:, first] * lm_jac[:, second], axis=(0, 1))

    w_00 = entry(0, 0) + DAMPING
    w_11 = entry(1, 1) + DAMPING
    w_22 = entry(2, 2) + DAMPING
    w_01 = entry(0, 1)
    w_02 = entry(0, 2)
    w_12 = entry(1, 2)
    cof_00 = w_11 * w_22 - w_12 * w_12
    cof_01 = w_02 * w_12 - w_01 * w_22
    cof_02 = w_01 * w_12 - w_02 * w_11
    cof_11 = w_00 * w_22 - w_02 * w_02
    cof_12 = w_01 * w_02 - w_00 * w_12
    cof_22 = w_00 * w_11 - w_01 * w_01
    determinant = w_00 * cof_00 + w_01 * cof_01 + w_02 * cof_02
    rows = [
        jnp.stack([cof_00, cof_01, cof_02]),
        jnp.stack([cof_01, cof_11, cof_12]),
        jnp.stack([cof_02, cof_12, cof_22]),
    ]
    return jnp.stack(rows) / determinant[None, None]


def apply_inverse(inverse, vector):
    return jnp.sum(inverse * vector[None], axis=1)


def landmark_side(lm_jac, values):
    return jnp.sum(lm_jac * values[:, None], axis=(0, 2))


def back_project(lm_jac, landmark):
    return jnp.sum(lm_jac * landmark[None, :, None, :], axis=1)


def camera_apply(cam_jac, cam_values):
    return jnp.sum(cam_jac * cam_values[None], axis=1)


def camera_transpose(cam_jac, errors):
    return jnp.sum(cam_jac * errors[:, None], axis=0)


def to_cameras(values, cam_index, total_cams):
    flat_index = cam_index.reshape(-1)
    width = values.shape[0]

    def one_row(column):
        return jax.ops.segment_sum(column, flat_index, num_segments=total_cams)

    return jax.vmap(one_row)(values.reshape(width, -1))


def schur_obs(cam_jac, lm_jac, inverse, cam_values):
    applied = camera_apply(cam_jac, cam_values)
    landmark = apply_inverse(inverse, landmark_side(lm_jac, applied))
    return camera_transpose(cam_jac, applied - back_project(lm_jac, landmark))


def gather_cameras(tile):
    return lax.all_gather(tile, "dev", axis=1, tiled=True)


def reduce_cameras(terms):
    totals = lax.psum(terms, ("group", "dev"))
    width = terms.shape[1] // lax.axis_size("dev")
    return lax.dynamic_slice_in_dim(totals, lax.axis_index("dev") * width, width, 1)


def inner_product(left, right):
    return lax.psum(jnp.sum(left * right), "dev")


def body(cam_jac, lm_jac, resid, cam_index):
    total_cams = CAM_DEV * lax.axis_size("dev")
    inverse = landmark_inverse(lm_jac)
    land_rhs = apply_inverse(inverse, landmark_side(lm_jac, resid))
    errors = resid - back_project(lm_jac, land_rhs)
    stacked = jnp.concatenate(
        [camera_transpose(cam_jac, errors), jnp.sum(cam_jac * cam_jac, axis=0)], axis=0
    )
    summed = reduce_cameras(to_cameras(stacked, cam_index, total_cams))
    gradient = summed[:9]
    diagonal = summed[9:] + DAMPING
    residual = gradient
    precond = residual / diagonal
    direction = precond
    rz_now = inner_product(residual, precond)
    solution = jnp.zeros_like(gradient)
    for iteration in range(ITERS):
        whole = gather_cameras(direction)
        cam_values = jnp.take(whole, cam_index, axis=1)
        terms = to_cameras(schur_obs(cam_jac, lm_jac, inverse, cam_values), cam_index, total_cams)
        image = reduce_cameras(terms) + DAMPING * direction
        alpha = rz_now / inner_product(direction, image)
        solution = solution + alpha * direction
        residual = residual - alpha * image
        if iteration + 1 < ITERS:
            precond = residual / diagonal
            rz_next = inner_product(residual, precond)
            direction = precond + rz_next / rz_now * direction
            rz_now = rz_next
    whole_step = gather_cameras(solution)
    cam_obs = camera_apply(cam_jac, jnp.take(whole_step, cam_index, axis=1))
    landmark_step = land_rhs - apply_inverse(inverse, landmark_side(lm_jac, cam_obs))
    return (solution, residual, landmark_step)


def solution(mesh):
    in_specs = (
        P(None, None, None, ("group", "dev")),
        P(None, None, None, ("group", "dev")),
        P(None, None, ("group", "dev")),
        P(None, ("group", "dev")),
    )
    out_specs = (P(None, "dev"), P(None, "dev"), P(None, ("group", "dev")))
    return jax.shard_map(body, mesh=mesh, in_specs=in_specs, out_specs=out_specs, check_vma=False)
```

profile of v0, /device:TPU:8, one launch (start us, length us, event | category | flops | bytes accessed | tf_op | source)
XLA Modules:
  0.0 2390.0 jit_solution(14837299796872105308)
XLA Ops:
  7.2 0.8 multiply_reduce_fusion.22
  8.0 0.9 multiply_reduce_fusion.13
  9.0 0.7 copy.31
  9.8 0.9 multiply_reduce_fusion.12
  10.7 0.8 sub.128
  11.5 1.0 multiply_reduce_fusion.6
  13.2 24.5 %scatter_custom_fusion = f32[18,8192]{0,1:T(8,128)} fusion(s32[4096]{0:T(1024)S(1)} %bitcast.43, f32[4096,18]{1,0:T(8,128)S(1)} %bitcast.38, f32[]{:T(128)} %constant.14.clone.1), kind=kCustom, calls=%fused_computation.13 | custom fusion | flops 73728 | bytes 589828 | tf_op jit(solution)/shard_map/vmap()/scatter-add | solution.py:62
  37.9 494.2 %all-reduce.5.cloned.1.call-done = f32[18,8192]{0,1:T(8,128)} async-done(((f32[18,8192]{0,1:T(8,128)}), f32[18,8192]{0,1:T(8,128)}) %all-reduce.5.cloned.1.call-update) | async-done | bytes 589840 | tf_op jit(solution)/shard_map/psum | solution.py:78
  532.1 1.0 fusion.7
  533.1 111.9 %all_gather.9 = f32[9,8192]{0,1:T(8,128)} all-gather(f32[9,128]{0,1:T(8,128)S(1)} %fusion.7), channel_id=1, replica_groups=mesh['group'=8,'dev'=64] {'dev'}, dimensions={1}, use_global_device_ids=true | all-gather | bytes 299520 | tf_op jit(solution)/shard_map/all_gather | solution.py:74
  645.0 16.3 gather_fusion
  661.3 1.9 select_bitcast_fusion.2
  664.8 24.5 %scatter_custom_fusion.1 = f32[9,8192]{0,1:T(8,128)} fusion(s32[4096]{0:T(1024)S(1)} %bitcast.44, f32[4096,9]{1,0:T(8,128)S(1)} %bitcast.40, f32[]{:T(128)} %constant.14.clone.1), kind=kCustom, calls=%fused_computation.11 | custom fusion | flops 36864 | bytes 294916 | tf_op jit(solution)/shard_map/vmap()/scatter-add | solution.py:62
  689.4 488.0 %all-reduce.7.cloned.1.call-done = f32[9,8192]{0,1:T(8,128)} async-done(((f32[9,8192]{0,1:T(8,128)}), f32[9,8192]{0,1:T(8,128)}) %all-reduce.7.cloned.1.call-update) | async-done | bytes 294928 | tf_op jit(solution)/shard_map/psum | solution.py:78
  1177.4 1.6 multiply_reduce_fusion.16
  1179.0 139.5 %all-reduce = (f32[]{:T(128)}, f32[]{:T(128)}) all-reduce(f32[]{:T(128)} %get-tuple-element.22, f32[]{:T(128)} %get-tuple-element.21), channel_id=1, replica_groups=mesh['group'=8,'dev'=64] {'dev'}, use_global_device_ids=true, to_apply=%region_14.0 | all-reduce | flops 2 | bytes 16 | tf_op jit(solution)/shard_map/psum | solution.py:84
  1319.8 1.6 multiply_reduce_fusion.15
  1321.4 140.7 %psum.53 = f32[]{:T(128)} all-reduce(f32[]{:T(128)} %get-tuple-element.25), channel_id=1, replica_groups=mesh['group'=8,'dev'=64] {'dev'}, use_global_device_ids=true, to_apply=%region_25.27 | all-reduce | flops 1 | bytes 8 | tf_op jit(solution)/shard_map/psum | solution.py:84
  1463.5 1.0 multiply_add_fusion.1
  1464.5 110.5 %all_gather.10 = f32[9,8192]{0,1:T(8,128)} all-gather(f32[9,128]{0,1:T(8,128)S(1)} %multiply_add_fusion.1), channel_id=1, replica_groups=mesh['group'=8,'dev'=64] {'dev'}, dimensions={1}, use_global_device_ids=true | all-gather | bytes 299520 | tf_op jit(solution)/shard_map/all_gather | solution.py:74
  1575.0 16.3 gather_fusion.1
  1591.2 1.9 select_bitcast_fusion.1
  1594.6 24.5 %scatter_custom_fusion.2 = f32[9,8192]{0,1:T(8,128)} fusion(s32[4096]{0:T(1024)S(1)} %bitcast.45, f32[4096,9]{1,0:T(8,128)S(1)} %bitcast.39, f32[]{:T(128)} %constant.14.clone.1), kind=kCustom, calls=%fused_computation.9 | custom fusion | flops 36864 | bytes 294916 | tf_op jit(solution)/shard_map/vmap()/scatter-add | solution.py:62
  1619.2 488.2 %all-reduce.9.cloned.1.call-done = f32[9,8192]{0,1:T(8,128)} async-done(((f32[9,8192]{0,1:T(8,128)}), f32[9,8192]{0,1:T(8,128)}) %all-reduce.9.cloned.1.call-update) | async-done | bytes 294928 | tf_op jit(solution)/shard_map/psum | solution.py:78
  2107.4 1.5 multiply_reduce_fusion.14
  2108.9 139.4 %psum.55 = f32[]{:T(128)} all-reduce(f32[]{:T(128)} %multiply_reduce_fusion.14), channel_id=1, replica_groups=mesh['group'=8,'dev'=64] {'dev'}, use_global_device_ids=true, to_apply=%region_34.36 | all-reduce | flops 1 | bytes 8 | tf_op jit(solution)/shard_map/psum | solution.py:84
  2249.7 1.0 multiply_subtract_fusion
  2250.7 0.7 copy.26
  2251.4 111.8 %all_gather.11 = f32[9,8192]{0,1:T(8,128)} all-gather(f32[9,128]{0,1:T(8,128)S(1)} %get-tuple-element.34), channel_id=1, replica_groups=mesh['group'=8,'dev'=64] {'dev'}, dimensions={1}, use_global_device_ids=true | all-gather | bytes 299520 | tf_op jit(solution)/shard_map/all_gather | solution.py:74
  2363.2 0.7 copy.27
  2363.9 16.3 gather_fusion.2
  2380.2 1.9 select_bitcast_fusion
  (42 shorter events, 5.1 us)
Async XLA Ops:
  7.2 524.9 %all-reduce.5.cloned.1.call-start = ((), (), s32[]{:S(2)}) async-start(), calls=%async_computation | async-start | bytes 8388608 | tf_op jit(solution)/shard_map/psum | solution.py:78
  13.2 24.6 %copy-start.2 = (s32[8,512]{1,0:T(8,128)S(1)}, s32[8,512]{1,0:T(8,128)}, u32[]{:S(2)}) copy-start(s32[8,512]{1,0:T(8,128)} %param.9) | copy-start | bytes 49156
  37.8 1139.6 %all-reduce.7.cloned.1.call-start = ((), (), s32[]{:S(2)}) async-start(), calls=%async_computation.1 | async-start | bytes 8388608 | tf_op jit(solution)/shard_map/psum | solution.py:78
  645.0 18.9 copy-start
  645.0 19.0 copy-start.1
  689.3 1418.1 %all-reduce.9.cloned.1.call-start = ((), (), s32[]{:S(2)}) async-start(), calls=%async_computation.2 | async-start | bytes 8388608 | tf_op jit(solution)/shard_map/psum | solution.py:78
Sparse Core Ops, SparseCore 0:
  37.9 494.1 all-reduce.4
  689.4 487.8 all-reduce.6
  1619.3 488.0 all-reduce.8
where the time goes:
time: 2390 us
  waiting for transfers between devices  1470 us (62%)
  blocking collectives  754 us (32%)
  other arithmetic  92.8 us (4%)
  local copies, waits for them, and re-layouts  54.8 us (2%)
    psum x3, waiting for transfers between devices, reduce_cameras(): totals = lax.psum(terms, ('group', 'dev'))  1470 us
    psum x3, blocking collectives, inner_product(): return lax.psum(jnp.sum(left * right), 'dev')  420 us
    all_gather x3, blocking collectives, gather_cameras(): return lax.all_gather(tile, 'dev', axis=1, tiled=True)  334 us
    scatter-add x3, other arithmetic, one_row(): return jax.ops.segment_sum(column, flat_index, num_segments=total_cams)  73.6 us
  transfers between devices with their start and end apart: 3, of which 3 were waited for; matrix products, arithmetic and copies ran while one was open for 0% of the time, Pallas kernels for 0%

commit v1 on v0

--- a/solution.py
+++ b/solution.py
@@ -6,6 +6,18 @@
 CAM_DEV = 128
 ITERS = 2
 DAMPING = 1.0
+
+
+def gather_by_bits(x, axis, dim):
+    ways, here = (lax.axis_size(axis), lax.axis_index(axis))
+    grown, reach = (x, 1)
+    while reach < ways:
+        theirs = lax.ppermute(grown, axis, [(d, d ^ reach) for d in range(ways)])
+        mine_first = jnp.concatenate([grown, theirs], axis=dim)
+        theirs_first = jnp.concatenate([theirs, grown], axis=dim)
+        grown = jnp.where(here & reach == 0, mine_first, theirs_first)
+        reach = 2 * reach
+    return grown
 
 
 def landmark_inverse(lm_jac):
@@ -71,7 +83,7 @@
 
 
 def gather_cameras(tile):
-    return lax.all_gather(tile, "dev", axis=1, tiled=True)
+    return gather_by_bits(tile, "dev", 1)
 
 
 def reduce_cameras(terms):

time: 2390 us -> 2210 us (0.925)
  the two profiles are of different devices: /device:TPU:8 before, /device:TPU:6 now
where the time goes in v1:
time: 2210 us
  waiting for transfers between devices  1520 us (69%)
  blocking collectives  420 us (19%)
  other arithmetic  106 us (5%)
  local copies, waits for them, and re-layouts  79.9 us (4%)
  starting transfers between devices  70.9 us (3%)
    psum x3, waiting for transfers between devices, reduce_cameras(): totals = lax.psum(terms, ('group', 'dev'))  1390 us
    psum x3, blocking collectives, inner_product(): return lax.psum(jnp.sum(left * right), 'dev')  420 us
    ppermute x18, waiting for transfers between devices, gather_by_bits(): theirs = lax.ppermute(grown, axis, [(d, d ^ reach) for d in range(ways)])  126 us
    scatter-add x3, other arithmetic, one_row(): return jax.ops.segment_sum(column, flat_index, num_segments=total_cams)  73.5 us
    ppermute x18, starting transfers between devices, gather_by_bits(): theirs = lax.ppermute(grown, axis, [(d, d ^ reach) for d in range(ways)])  70.8 us
  transfers between devices with their start and end apart: 21, of which 21 were waited for; matrix products, arithmetic and copies ran while one was open for 0% of the time, Pallas kernels for 0%

profile of v1, /device:TPU:6, one launch (start us, length us, event | category | flops | bytes accessed | tf_op | source)
XLA Modules:
  0.0 2211.8 jit_solution(1200947291117172686)
XLA Ops:
  13.2 24.5 %scatter_custom_fusion = f32[18,8192]{0,1:T(8,128)} fusion(s32[4096]{0:T(1024)S(1)} %bitcast.43, f32[4096,18]{1,0:T(8,128)S(1)} %bitcast.38, f32[]{:T(128)} %constant.20.clone.1), kind=kCustom, calls=%fused_computation.13 | custom fusion | flops 73728 | bytes 589828 | tf_op jit(solution)/shard_map/vmap()/scatter-add | solution.py:74
  41.4 473.0 %all-reduce.5.cloned.1.call-done = f32[18,8192]{1,0:T(8,128)} async-done(((f32[18,8192]{1,0:T(8,128)}), f32[18,8192]{1,0:T(8,128)}) %all-reduce.5.cloned.1.call-update) | async-done | bytes 589840 | tf_op jit(solution)/shard_map/psum | solution.py:90
  535.7 5.2 collective-permute-done.3
  540.9 5.3 collective-permute-start.4
  546.2 10.0 collective-permute-done.4
  556.2 9.1 collective-permute-start.5
  565.4 21.7 collective-permute-done.5
  592.4 4.6 broadcast_select_fusion.2
  597.0 16.3 gather_fusion
  616.7 24.5 %scatter_custom_fusion.1 = f32[9,8192]{0,1:T(8,128)} fusion(s32[4096]{0:T(1024)S(1)} %bitcast.44, f32[4096,9]{1,0:T(8,128)S(1)} %bitcast.40, f32[]{:T(128)} %constant.20.clone.1), kind=kCustom, calls=%fused_computation.11 | custom fusion | flops 36864 | bytes 294916 | tf_op jit(solution)/shard_map/vmap()/scatter-add | solution.py:74
  644.9 454.8 %all-reduce.7.cloned.1.call-done = f32[9,8192]{1,0:T(8,128)} async-done(((f32[9,8192]{1,0:T(8,128)}), f32[9,8192]{1,0:T(8,128)}) %all-reduce.7.cloned.1.call-update) | async-done | bytes 294928 | tf_op jit(solution)/shard_map/psum | solution.py:90
  1101.2 140.5 %all-reduce = (f32[]{:T(128)}, f32[]{:T(128)}) all-reduce(f32[]{:T(128)} %get-tuple-element.22, f32[]{:T(128)} %get-tuple-element.21), channel_id=1, replica_groups=mesh['group'=8,'dev'=64] {'dev'}, use_global_device_ids=true, to_apply=%region_14.0 | all-reduce | flops 2 | bytes 16 | tf_op jit(solution)/shard_map/psum | solution.py:96
  1244.4 139.4 %psum.53 = f32[]{:T(128)} all-reduce(f32[]{:T(128)} %get-tuple-element.25), channel_id=1, replica_groups=mesh['group'=8,'dev'=64] {'dev'}, use_global_device_ids=true, to_apply=%region_25.27 | all-reduce | flops 1 | bytes 8 | tf_op jit(solution)/shard_map/psum | solution.py:96
  1393.5 5.2 collective-permute-done.7
  1406.5 5.3 collective-permute-done.9
  1411.8 6.3 collective-permute-start.10
  1418.1 7.9 collective-permute-done.10
  1426.1 9.1 collective-permute-start.11
  1435.2 8.1 collective-permute-done.11
  1448.7 4.6 broadcast_select_fusion.1
  1453.3 16.3 gather_fusion.1
  1472.9 24.5 %scatter_custom_fusion.2 = f32[9,8192]{0,1:T(8,128)} fusion(s32[4096]{0:T(1024)S(1)} %bitcast.45, f32[4096,9]{1,0:T(8,128)S(1)} %bitcast.39, f32[]{:T(128)} %constant.20.clone.1), kind=kCustom, calls=%fused_computation.9 | custom fusion | flops 36864 | bytes 294916 | tf_op jit(solution)/shard_map/vmap()/scatter-add | solution.py:74
  1501.0 461.8 %all-reduce.9.cloned.1.call-done = f32[9,8192]{1,0:T(8,128)} async-done(((f32[9,8192]{1,0:T(8,128)}), f32[9,8192]{1,0:T(8,128)}) %all-reduce.9.cloned.1.call-update) | async-done | bytes 294928 | tf_op jit(solution)/shard_map/psum | solution.py:90
  1964.1 140.4 %psum.55 = f32[]{:T(128)} all-reduce(f32[]{:T(128)} %multiply_reduce_fusion.24), channel_id=1, replica_groups=mesh['group'=8,'dev'=64] {'dev'}, use_global_device_ids=true, to_apply=%region_34.36 | all-reduce | flops 1 | bytes 8 | tf_op jit(solution)/shard_map/psum | solution.py:96
  2114.8 5.2 collective-permute-done.13
  2121.9 5.7 collective-permute-done.14
  2129.5 6.4 collective-permute-done.15
  2139.1 11.6 collective-permute-done.16
  2150.7 9.7 collective-permute-start.17
  2160.4 15.3 collective-permute-done.17
  2181.1 4.6 broadcast_select_fusion
  2185.7 16.3 gather_fusion.2
  (105 shorter events, 100.3 us)
Async XLA Ops:
  7.2 507.2 %all-reduce.5.cloned.1.call-start = ((), (), s32[]{:S(2)}) async-start(), calls=%async_computation | async-start | bytes 1572864 | tf_op jit(solution)/shard_map/psum | solution.py:90
  13.2 522.5 %copy-start.2 = (s32[8,512]{1,0:T(8,128)S(1)}, s32[8,512]{1,0:T(8,128)}, u32[]{:S(2)}) copy-start(s32[8,512]{1,0:T(8,128)} %param.9) | copy-start | bytes 49156
  41.3 1058.4 %all-reduce.7.cloned.1.call-start = ((), (), s32[]{:S(2)}) async-start(), calls=%async_computation.1 | async-start | bytes 1048576 | tf_op jit(solution)/shard_map/psum | solution.py:90
  515.2 5.5 collective-permute-start
  520.8 7.1 collective-permute-start.1
  527.9 5.8 collective-permute-start.2
  533.7 7.2 collective-permute-start.3
  540.9 15.3 collective-permute-start.4
  556.2 30.8 %collective-permute-start.5 = (f32[9,4096]{1,0:T(8,128)S(1)}, f32[9,4096]{1,0:T(8,128)S(1)}, u32[]{:S(2)}, u32[]{:S(2)}) collective-permute-start(f32[9,4096]{1,0:T(8,128)S(1)} %maximum_select_fusion), channel_id=1, source_target_pairs={{0,32},{1,33},{2,34},{3,35},{4,36},{5,37},{6,38},{7,39},{8,40},{9,... | collective-permute-start | bytes 442376 | tf_op jit(solution)/shard_map/ppermute | solution.py:15
  597.0 18.9 copy-start
  597.0 18.9 copy-start.1
  644.8 1318.0 %all-reduce.9.cloned.1.call-start = ((), (), s32[]{:S(2)}) async-start(), calls=%async_computation.2 | async-start | bytes 1048576 | tf_op jit(solution)/shard_map/psum | solution.py:90
  1386.1 5.5 collective-permute-start.6
  1391.6 7.1 collective-permute-start.7
  1398.7 5.8 collective-permute-start.8
  1404.6 7.2 collective-permute-start.9
  1411.8 14.3 collective-permute-start.10
  1426.1 17.2 collective-permute-start.11
  2107.3 73.8 %copy-start.3 = (f32[9,128]{1,0:T(8,128)}, f32[9,128]{1,0:T(8,128)S(1)}, u32[]{:S(2)}) copy-start(f32[9,128]{1,0:T(8,128)S(1)} %get-tuple-element.40) | copy-start | bytes 13828
  2107.3 5.5 collective-permute-start.12
  2112.8 7.1 collective-permute-start.13
  2120.0 7.6 collective-permute-start.14
  2127.6 8.3 collective-permute-start.15
  2135.9 14.8 collective-permute-start.16
  2150.7 25.0 %collective-permute-start.17 = (f32[9,4096]{1,0:T(8,128)S(1)}, f32[9,4096]{1,0:T(8,128)S(1)}, u32[]{:S(2)}, u32[]{:S(2)}) collective-permute-start(f32[9,4096]{1,0:T(8,128)S(1)} %maximum_select_fusion.2), channel_id=1, source_target_pairs={{0,32},{1,33},{2,34},{3,35},{4,36},{5,37},{6,38},{7,39},{8,40},{9,... | collective-permute-start | bytes 442376 | tf_op jit(solution)/shard_map/ppermute | solution.py:15
Sparse Core Ops, SparseCore 0:
  41.4 472.9 all-reduce.4
  644.9 454.7 all-reduce.6
  1501.1 461.6 all-reduce.8
